TPU v7x, 32 devices: a whole 2x2x4 slice. The times are simulated.
32 devices in a mesh: dp: 2 (over y), row: 2 (over core), col: 8 (over z, x).
Axes of the slice: x: 2, y: 2, z: 4, core: 2. Of those that a mesh axis runs over, the one named last changes fastest.
Arguments:
- gate_pre: bfloat16 [512, 28672], P(('dp', 'row'), 'col'), may hold values from -6 to 6
- up_pre: bfloat16 [512, 28672], P(('dp', 'row'), 'col'), may hold values from -6 to 6
- grad_out: bfloat16 [512, 16384], P('col', ('dp', 'row')), may hold values from -6 to 6
- down_weight: bfloat16 [28672, 16384], P('col', ('dp', 'row')), may hold values from -0.046875 to 0.046875
- basis: bfloat16 [512, 28672], P(('dp', 'row'), 'col'), may hold values from -0.046875 to 0.046875
- first_moment_in: float32 [512, 16384], P('col', ('dp', 'row')), may hold values from -6 to 6
- second_moment_in: float32 [512, 16384], P('col', ('dp', 'row')), may hold values from 0.1 to 10
Outputs:
- grad_gate: bfloat16 [512, 28672], P(('dp', 'row'), 'col')
- grad_up: bfloat16 [512, 28672], P(('dp', 'row'), 'col')
- scaled_grad: bfloat16 [28672, 16384], P('col', ('dp', 'row'))
- first_moment: float32 [512, 16384], P('col', ('dp', 'row'))
- second_moment: float32 [512, 16384], P('col', ('dp', 'row'))
All inputs are finite; a program needn't handle non-finite values.
Results may differ from a plain program's by a relative error of at most 0.024.
Values may be sent and summed in bfloat16 or wider, within the bound.
A program may use at most 128 MiB of HBM per device.

v0:
```python
import math

import jax
import jax.numpy as jnp
from jax import lax
from jax.sharding import PartitionSpec as P

first_fix = 1.0 - math.exp(1000.0 * math.log(0.9))
second_fix = 1.0 - math.exp(1000.0 * math.log(0.999))


def adam_rows(first_in, second_in, projected):
    first_new = 0.9 * first_in + 0.1 * projected
    second_new = 0.999 * second_in + 0.001 * projected * projected
    adapted = first_new / first_fix / (jnp.sqrt(second_new / second_fix) + 1e-06)
    return (first_new, second_new, adapted)


def shards(gate_pre, up_pre, grad_out, down_weight, basis, first_moment_in, second_moment_in):
    gate_f = gate_pre.astype(jnp.float32)
    up_f = up_pre.astype(jnp.float32)
    sigma = jax.nn.sigmoid(gate_f)
    act_value = gate_f * sigma
    hidden = (act_value * up_f).astype(jnp.bfloat16)
    cotangent = lax.all_gather(grad_out, "col", axis=0, tiled=True)
    out_rows = cotangent
    summed = lax.psum_scatter(
        lax.dot_general(
            out_rows, down_weight, (((1,), (1,)), ((), ())), preferred_element_type=jnp.float32
        ).astype(jnp.bfloat16),
        ("dp", "row"),
        scatter_dimension=0,
        tiled=True,
    )
    grad_hidden = summed.astype(jnp.float32)
    grad_up = (grad_hidden * act_value).astype(jnp.bfloat16)
    grad_gate = (grad_hidden * up_f * sigma * (1.0 + gate_f * (1.0 - sigma))).astype(jnp.bfloat16)
    out_rows = cotangent
    weight_exact = lax.dot_general(
        lax.all_gather(hidden, ("dp", "row"), axis=0, tiled=True),
        out_rows,
        (((0,), (0,)), ((), ())),
        preferred_element_type=jnp.float32,
    )
    grad_weight = weight_exact.astype(jnp.bfloat16)
    basis_full = lax.all_gather(basis, ("dp", "row"), axis=0, tiled=True)
    own_tokens = lax.psum_scatter(
        lax.dot_general(
            basis_full, hidden, (((1,), (1,)), ((), ())), preferred_element_type=jnp.float32
        ).astype(jnp.bfloat16),
        "col",
        scatter_dimension=0,
        tiled=True,
    ).astype(jnp.float32)
    every_token = lax.all_gather(own_tokens, ("dp", "row"), axis=1, tiled=True)
    projected = jnp.dot(every_token, cotangent.astype(jnp.float32), precision=lax.Precision.HIGHEST)
    first_moment, second_moment, adapted = adam_rows(first_moment_in, second_moment_in, projected)
    adapted_sq, projected_sq = lax.psum(
        (jnp.sum(adapted * adapted, axis=0), jnp.sum(projected * projected, axis=0)), "col"
    )
    column_scale = jnp.sqrt(adapted_sq) / (jnp.sqrt(projected_sq) + 1e-06)
    scaled_grad = (grad_weight.astype(jnp.float32) * column_scale[None, :]).astype(jnp.bfloat16)
    return (grad_gate, grad_up, scaled_grad, first_moment, second_moment)


def solution(mesh):
    placed = (
        P(("dp", "row"), "col"),
        P(("dp", "row"), "col"),
        P("col", ("dp", "row")),
        P("col", ("dp", "row")),
        P(("dp", "row"), "col"),
        P("col", ("dp", "row")),
        P("col", ("dp", "row")),
    )
    return jax.shard_map(
        shards,
        mesh=mesh,
        in_specs=placed,
        out_specs=(
            P(("dp", "row"), "col"),
            P(("dp", "row"), "col"),
            P("col", ("dp", "row")),
            P("col", ("dp", "row")),
            P("col", ("dp", "row")),
        ),
        check_vma=False,
    )
```

profile of v0, /device:TPU:0, one launch (start us, length us, event | category | flops | bytes accessed | tf_op | source)
XLA Modules:
  0.0 323.9 jit_solution(17090805394841380071)
XLA Ops:
  7.2 0.0 all-gather.4.cloned.1.call-start
  7.2 0.7 all-gather.4.cloned.1.call-update
  7.9 0.0 reduce-scatter.5.cloned.1.call-start
  7.9 78.3 %all-gather.4.cloned.1.call-done = bf16[512,4096]{1,0:T(8,128)(2,1)} async-done(((bf16[64,4096]{1,0:T(8,128)(2,1)}), bf16[512,4096]{1,0:T(8,128)(2,1)}) %all-gather.4.cloned.1.call-update) | async-done | bytes 4194320 | tf_op jit(solution)/shard_map/all_gather | solution.py:25
  86.3 23.0 %convolution_convert_fusion.1 = bf16[512,3584]{1,0:T(8,128)(2,1)} fusion(bf16[512,4096]{1,0:T(8,128)(2,1)} %all-gather.4.cloned.1.call-done, bf16[3584,4096]{1,0:T(8,128)(2,1)} %param.10), kind=kOutput, calls=%fused_computation.2 | convolution fusion | flops 15034220544 | bytes 37224448 | tf_op jit(solution)/shard_map/dot_general | solution.py:28
  109.3 0.0 copy-start.1
  109.3 0.0 copy-start.2
  109.3 0.0 reduce-scatter.5.cloned.1.call-update
  109.3 0.0 all-gather.8.cloned.1.call-start
  109.3 0.7 all-gather.8.cloned.1.call-update
  110.0 0.0 reduce-scatter.7.cloned.1.call-start
  110.1 38.9 %reduce-scatter.5.cloned.1.call-done = bf16[128,3584]{1,0:T(8,128)(2,1)} async-done(((bf16[512,3584]{1,0:T(8,128)(2,1)}), bf16[128,3584]{1,0:T(8,128)(2,1)}) %reduce-scatter.5.cloned.1.call-update) | async-done | bytes 917520 | tf_op jit(solution)/shard_map/reduce_scatter | solution.py:27
  149.0 0.0 copy-done.1
  149.0 0.0 copy-done.2
  149.0 3.5 %fusion.4 = (bf16[128,3584]{1,0:T(8,128)(2,1)S(1)}, bf16[128,3584]{1,0:T(8,128)(2,1)}, bf16[128,3584]{1,0:T(8,128)(2,1)}) fusion(bf16[128,3584]{1,0:T(8,128)(2,1)S(1)} %copy-done.1, bf16[128,3584]{1,0:T(8,128)(2,1)S(1)} %copy-done.2, bf16[128,3584]{1,0:T(8,128)(2,1)} %reduce-scatter.5.cloned.1.call-done), kind=kLoop, calls=%fused_computation.13 | loop fusion | flops 8257536 | bytes 5505024 | tf_op jit(solution)/shard_map/convert_element_type | solution.py:24
  152.5 0.0 copy-start
  152.5 0.0 copy-start.3
  152.5 0.0 copy-start.4
  152.5 29.7 %all-gather.8.cloned.1.call-done = bf16[512,3584]{1,0:T(8,128)(2,1)} async-done(((bf16[128,3584]{1,0:T(8,128)(2,1)}), bf16[512,3584]{1,0:T(8,128)(2,1)}) %all-gather.8.cloned.1.call-update) | async-done | bytes 3670032 | tf_op jit(solution)/shard_map/all_gather | solution.py:46
  182.2 3.3 %fusion.9 = bf16[512,128]{0,1:T(8,128)(2,1)S(1)} fusion(bf16[128,3584]{1,0:T(8,128)(2,1)S(1)} %get-tuple-element.10, bf16[512,3584]{1,0:T(8,128)(2,1)} %all-gather.8.cloned.1.call-done), kind=kOutput, calls=%fused_computation.20 | convolution fusion | flops 469827584 | bytes 4718592 | tf_op jit(solution)/shard_map/dot_general | solution.py:48
  185.5 0.8 copy.12
  186.3 0.0 reduce-scatter.7.cloned.1.call-update
  186.3 0.0 all-gather.6.cloned.1.call-start
  186.3 0.0 copy-done
  186.3 0.5 all-gather.6.cloned.1.call-update
  186.9 60.5 %reduce-scatter.7.cloned.1.call-done = bf16[64,128]{1,0:T(8,128)(2,1)} async-done(((bf16[512,128]{1,0:T(8,128)(2,1)}), bf16[64,128]{1,0:T(8,128)(2,1)}) %reduce-scatter.7.cloned.1.call-update) | async-done | bytes 16400
  247.3 0.8 copy.13
  248.2 5.8 %all_gather.15 = f32[64,512]{0,1:T(8,128)S(1)} all-gather(f32[64,128]{0,1:T(8,128)S(1)} %convert_element_type.51), channel_id=1, replica_groups=mesh['dp'=2,'row'=2,'col'=8] {'dp','row'}, dimensions={1}, use_global_device_ids=true | all-gather | bytes 163840 | tf_op jit(solution)/shard_map/all_gather | solution.py:55
  254.0 0.0 copy-done.3
  254.0 0.0 copy-done.4
  254.0 6.9 %multiply_reduce_fusion.1 = (f32[4096]{0:T(1024)S(1)}, f32[64,4096]{1,0:T(8,128)}, f32[64,4096]{1,0:T(8,128)}, f32[4096]{0:T(1024)S(1)}) fusion(f32[64,4096]{1,0:T(8,128)S(1)} %copy-done.3, f32[64,4096]{1,0:T(8,128)S(1)} %copy-done.4, f32[64,512]{0,1:T(8,128)S(1)} %all_gather.15, bf16[512,4096]{1,0:T(8,128)(2,1)} %all-gather.4.cloned.1.call-done), kind=kOutput, calls=%fused_computation.23 | convolution fusion | flops 1614274560 | bytes 8552448 | tf_op jit(solution)/shard_map/dot_general | solution.py:56
  260.9 34.8 %all-reduce = (f32[4096]{0:T(1024)S(1)}, f32[4096]{0:T(1024)S(1)}) all-reduce(f32[4096]{0:T(1024)S(1)} %get-tuple-element.13, f32[4096]{0:T(1024)S(1)} %get-tuple-element.7), channel_id=1, replica_groups=mesh['dp'=2,'row'=2,'col'=8] {'col'}, use_global_device_ids=true, to_apply=%region_5.0 | all-reduce | flops 8192 | bytes 65536 | tf_op jit(solution)/shard_map/psum | solution.py:58
  295.7 0.0 all-gather.6.cloned.1.call-done
  295.7 21.7 %multiply_convert_fusion = bf16[3584,4096]{1,0:T(8,128)(2,1)} fusion(f32[4096]{0:T(1024)S(1)} %add_divide_fusion, bf16[512,3584]{1,0:T(8,128)(2,1)} %all-gather.6.cloned.1.call-done, bf16[512,4096]{1,0:T(8,128)(2,1)} %all-gather.4.cloned.1.call-done), kind=kOutput, calls=%fused_computation | convolution fusion | flops 15091105792 | bytes 37240832 | tf_op jit(solution)/shard_map/dot_general | solution.py:39
  (2 shorter events, 0.0 us)
Async XLA Ops:
  7.2 79.1 %all-gather.4.cloned.1.call-start = ((), (), s32[]{:S(2)}) async-start(), calls=%async_computation.2 | async-start | bytes 4718592 | tf_op jit(solution)/shard_map/all_gather | solution.py:25
  7.9 141.1 %reduce-scatter.5.cloned.1.call-start = ((), (), s32[]{:S(2)}) async-start(), calls=%async_computation.3 | async-start | bytes 4587520 | tf_op jit(solution)/shard_map/reduce_scatter | solution.py:27
  109.3 39.7 %copy-start.1 = (bf16[128,3584]{1,0:T(8,128)(2,1)S(1)}, bf16[128,3584]{1,0:T(8,128)(2,1)}, u32[]{:S(2)}) copy-start(bf16[128,3584]{1,0:T(8,128)(2,1)} %param.8) | copy-start | bytes 2752516
  109.3 39.7 %copy-start.2 = (bf16[128,3584]{1,0:T(8,128)(2,1)S(1)}, bf16[128,3584]{1,0:T(8,128)(2,1)}, u32[]{:S(2)}) copy-start(bf16[128,3584]{1,0:T(8,128)(2,1)} %param.7) | copy-start | bytes 2752516
  109.3 72.9 %all-gather.8.cloned.1.call-start = ((), (), s32[]{:S(2)}) async-start(), calls=%async_computation.5 | async-start | bytes 4587520 | tf_op jit(solution)/shard_map/all_gather | solution.py:46
  110.0 137.3 %reduce-scatter.7.cloned.1.call-start = ((), (), s32[]{:S(2)}) async-start(), calls=%async_computation.6 | async-start | bytes 147456
  152.5 33.8 %copy-start = (bf16[128,3584]{1,0:T(8,128)(2,1)}, bf16[128,3584]{1,0:T(8,128)(2,1)S(1)}, u32[]{:S(2)}) copy-start(bf16[128,3584]{1,0:T(8,128)(2,1)S(1)} %get-tuple-element.10) | copy-start | bytes 2752516
  152.5 101.5 %copy-start.3 = (f32[64,4096]{1,0:T(8,128)S(1)}, f32[64,4096]{1,0:T(8,128)}, u32[]{:S(2)}) copy-start(f32[64,4096]{1,0:T(8,128)} %param.13) | copy-start | bytes 3145732
  152.5 101.5 %copy-start.4 = (f32[64,4096]{1,0:T(8,128)S(1)}, f32[64,4096]{1,0:T(8,128)}, u32[]{:S(2)}) copy-start(f32[64,4096]{1,0:T(8,128)} %param.12) | copy-start | bytes 3145732
  186.3 109.5 %all-gather.6.cloned.1.call-start = ((), (), s32[]{:S(2)}) async-start(), calls=%async_computation.4 | async-start | bytes 4587520 | tf_op jit(solution)/shard_map/all_gather | solution.py:40
Sparse Core Ops, SparseCore 0:
  10.1 76.0 all-gather.3
  109.4 39.5 reduce-scatter.4
  150.6 31.5 all-gather.7
  186.4 60.8 reduce-scatter.6
  249.4 30.5 all-gather.5
where the time goes:
time: 324 us
  waiting for transfers between devices  209 us (65%)
  matrix products  54.9 us (17%)
  blocking collectives  40.6 us (13%)
  between operations  13.8 us (4%)
  other arithmetic  3.54 us (1%)
    all_gather x1, waiting for transfers between devices, shards(): cotangent = lax.all_gather(grad_out, 'col', axis=0, tiled=True)  78.3 us
    unnamed x6, waiting for transfers between devices  62.4 us
    reduce_scatter x1, waiting for transfers between devices, shards(): lax.psum_scatter(lax.dot_general(out_rows, down_weight, (((1,), (1,)), ((...  38.9 us
    psum x1, blocking collectives, shards(): lax.psum((jnp.sum(adapted * adapted, axis=0), jnp.sum(projected * project...  34.8 us
    all_gather x1, waiting for transfers between devices, shards(): basis_full = lax.all_gather(basis, ('dp', 'row'), axis=0, tiled=True)  29.7 us
    dot_general x1, matrix products, shards(): lax.dot_general(out_rows, down_weight, (((1,), (1,)), ((), ())), preferre...  23 us
    dot_general x1, matrix products, shards(): lax.dot_general(lax.all_gather(hidden, ('dp', 'row'), axis=0, tiled=True)...  21.7 us
    dot_general x1, matrix products, shards(): jnp.dot(every_token, cotangent.astype(jnp.float32), precision=lax.Precisi...  6.9 us
  transfers between devices with their start and end apart: 5, of which 4 were waited for; matrix products, arithmetic and copies ran while one was open for 3% of the time, Pallas kernels for 0%

commit v1 on v0

v1 whole, which is shorter than its diff:
```python
import functools
import math

import jax
import jax.numpy as jnp
from jax import lax
from jax.experimental import pallas as pl
from jax.experimental.pallas import tpu as pltpu
from jax.sharding import PartitionSpec as P

first_fix = 1.0 - math.exp(1000.0 * math.log(0.9))
second_fix = 1.0 - math.exp(1000.0 * math.log(0.999))

CONTRACT_LAST = (((1,), (1,)), ((), ()))


def width_of(extent, most):
    best = 128
    for width in range(128, most + 1, 128):
        if extent % width == 0:
            best = width
    return best


def remote(src, dst, send_sem, recv_sem, device):
    return pltpu.make_async_remote_copy(
        src_ref=src,
        dst_ref=dst,
        send_sem=send_sem,
        recv_sem=recv_sem,
        device_id=device,
        device_id_type=pl.DeviceIdType.MESH,
    )


def kernel(
    n_dp, n_row, n_col, tile, wide,
    gate, up, cot_in, weight, basis_in, first_in, second_in,
    grad_gate, grad_up, first_out, second_out, scale_out, cot_out, hid_out,
    cot, hid, basis, wt, part, recv1, half, recv2, tok_send, tok_recv, tok_all, sums,
    local_sem, w_sem, ring_s, ring_r, bas_s, bas_r, hid_s, hid_r, tk_s, tk_r,
    tg_s, tg_r, sum_s, sum_r, one_s, one_r, two_s, two_r,
):
    d, r, c = lax.axis_index("dp"), lax.axis_index("row"), lax.axis_index("col")
    group = n_dp * n_row
    k = d * n_row + r
    tokens, columns = cot.shape
    shard = tokens // n_col
    own = tokens // group
    units = hid.shape[1]
    ranks = basis.shape[0]
    own_ranks = ranks // group
    row_ranks = ranks // n_col
    tiles = units // tile
    hops = n_col // 2

    def around(me, offset, n):
        return lax.rem(me + offset + n, n)

    odd = lax.rem(c, 2)
    pos = (1 - odd) * lax.div(c, 2) + odd * (n_col - 1 - lax.div(c, 2))

    def at_pos(q):
        upper = lax.div(q, hops)
        return (1 - upper) * (2 * q) + upper * (2 * (n_col - 1 - q) + 1)

    def ring_col(offset):
        return at_pos(around(pos, offset, n_col))

    barrier = pltpu.get_barrier_semaphore()
    for o in range(1, n_col):
        pl.semaphore_signal(barrier, inc=1, device_id=(d, r, around(c, o, n_col)), device_id_type=pl.DeviceIdType.MESH)
    for o in range(1, n_row):
        pl.semaphore_signal(barrier, inc=1, device_id=(d, around(r, o, n_row), c), device_id_type=pl.DeviceIdType.MESH)
    for o in range(1, n_dp):
        pl.semaphore_signal(barrier, inc=1, device_id=(around(d, o, n_dp), r, c), device_id_type=pl.DeviceIdType.MESH)
    pl.semaphore_wait(barrier, n_col + n_row + n_dp - 3)

    sent = []

    def start(copy):
        copy.start()
        sent.append(copy)

    def rows_of(col_index):
        return cot.at[pl.ds(pl.multiple_of(col_index * shard, shard), shard)]

    def half_of(col_index, which):
        return cot.at[pl.ds(pl.multiple_of(col_index * shard + which * (shard // 2), shard // 2), shard // 2)]

    def ring_copy(step, way):
        sign = 1 - 2 * way
        source = ring_col(-sign * (step - 1))
        target = (d, r, ring_col(sign))
        if step == hops:
            dst = half_of(source, way)
            src = dst if step > 1 else cot_in.at[pl.ds(way * (shard // 2), shard // 2)]
        else:
            dst = rows_of(source)
            src = dst if step > 1 else cot_in
        return remote(src, dst, ring_s.at[way, step - 1], ring_r.at[way, step - 1], target)

    def ring_arrived(step, way):
        sign = 1 - 2 * way
        source = ring_col(-sign * step)
        ref = half_of(source, way) if step == hops else rows_of(source)
        remote(ref, ref, ring_s.at[way, step - 1], ring_r.at[way, step - 1], (d, r, ring_col(sign))).wait_recv()

    def gather_start(src, slot, send, recv):
        for o in range(1, n_dp):
            start(remote(src, slot(k), send.at[o - 1], recv.at[k], (around(d, o, n_dp), r, c)))
        for o in range(1, n_row):
            start(remote(src, slot(k), send.at[n_dp - 1 + o - 1], recv.at[k], (d, around(r, o, n_row), c)))

    def gather_pass(slot, send, recv):
        for j in range(1, n_dp):
            block = around(d, -j, n_dp) * n_row + r
            remote(slot(block), slot(block), send.at[0], recv.at[block], (around(d, j, n_dp), r, c)).wait_recv()
            for o in range(1, n_row):
                start(remote(
                    slot(block), slot(block), send.at[n_dp - 1 + j * (n_row - 1) + o - 1], recv.at[block],
                    (d, around(r, o, n_row), c),
                ))

    def gather_end(slot, send, recv):
        for j in range(n_dp):
            for o in range(1, n_row):
                block = around(d, -j, n_dp) * n_row + around(r, -o, n_row)
                remote(slot(block), slot(block), send.at[0], recv.at[block], (d, around(r, o, n_row), c)).wait_recv()

    def basis_slot(block):
        return basis.at[pl.ds(pl.multiple_of(block * own_ranks, own_ranks), own_ranks)]

    def hid_slot(block):
        return hid.at[pl.ds(pl.multiple_of(block * own, own), own)]

    def tok_slot(block):
        return tok_all.at[block]

    start(ring_copy(1, 0))
    start(ring_copy(1, 1))
    gather_start(basis_in, basis_slot, bas_s, bas_r)
    own_cot = pltpu.make_async_copy(cot_in, rows_of(c), local_sem.at[0])
    own_cot.start()
    own_basis = pltpu.make_async_copy(basis_in, basis_slot(k), local_sem.at[1])
    own_basis.start()

    def weight_copy(t):
        return pltpu.make_async_copy(
            weight.at[pl.ds(pl.multiple_of(t * tile, tile), tile)], wt.at[t], w_sem.at[t])

    for t in range(tiles):
        weight_copy(t).start()

    @pl.loop(0, tiles)
    def _(t):
        at = pl.ds(pl.multiple_of(t * tile, tile), tile)
        gate_f = gate[:, at].astype(jnp.float32)
        act = gate_f * jax.nn.sigmoid(gate_f)
        hid[pl.ds(pl.multiple_of(k * own, own), own), at] = (act * up[:, at].astype(jnp.float32)).astype(jnp.bfloat16)

    step = 1

    def ring_step():
        nonlocal step
        if step > hops:
            return
        for way in (0, 1):
            ring_arrived(step, way)
            if step < hops:
                start(ring_copy(step + 1, way))
        step += 1

    ring_step()
    gather_pass(basis_slot, bas_s, bas_r)
    gather_start(hid_slot(k), hid_slot, hid_s, hid_r)
    own_basis.wait()
    gather_end(basis_slot, bas_s, bas_r)

    token_part = lax.dot_general(
        basis[...], hid[pl.ds(pl.multiple_of(k * own, own), own)], CONTRACT_LAST,
        preferred_element_type=jnp.float32)
    for j in range(n_col):
        tok_send[j] = token_part[j * row_ranks:(j + 1) * row_ranks].astype(jnp.bfloat16)
    for o in range(1, n_col):
        peer = around(c, o, n_col)
        start(remote(tok_send.at[peer], tok_recv.at[c], tk_s.at[o - 1], tk_r.at[c], (d, r, peer)))
    ring_step()
    total = tok_send[c].astype(jnp.float32)
    for o in range(1, n_col):
        peer = around(c, -o, n_col)
        remote(tok_recv.at[peer], tok_recv.at[peer], tk_s.at[o - 1], tk_r.at[peer], (d, r, around(c, o, n_col))).wait_recv()
        total = total + tok_recv[peer].astype(jnp.float32)
    tok_all[k] = total.astype(jnp.bfloat16)
    gather_start(tok_slot(k), tok_slot, tg_s, tg_r)
    ring_step()
    gather_pass(tok_slot, tg_s, tg_r)
    gather_end(tok_slot, tg_s, tg_r)
    while step <= hops:
        ring_step()
    own_cot.wait()
    cot_write = pltpu.make_async_copy(cot, cot_out, local_sem.at[2])
    cot_write.start()
    gather_pass(hid_slot, hid_s, hid_r)

    token_all = jnp.concatenate([tok_all[j] for j in range(group)], axis=1)

    @pl.loop(0, columns // wide)
    def _(j):
        at = pl.ds(pl.multiple_of(j * wide, wide), wide)
        projected = jnp.dot(token_all, cot[:, at], preferred_element_type=jnp.float32)
        first = 0.9 * first_in[:, at] + 0.1 * projected
        second = 0.999 * second_in[:, at] + 0.001 * projected * projected
        adapted = first / first_fix / (jnp.sqrt(second / second_fix) + 1e-06)
        first_out[:, at] = first
        second_out[:, at] = second
        sums[c, 0:1, at] = jnp.sum(adapted * adapted, axis=0, keepdims=True)
        sums[c, 1:2, at] = jnp.sum(projected * projected, axis=0, keepdims=True)

    for o in range(1, n_col):
        start(remote(sums.at[c], sums.at[c], sum_s.at[o - 1], sum_r.at[c], (d, r, around(c, o, n_col))))

    def one_copy(t, o):
        peer = around(r, o, n_row)
        return remote(part.at[t, peer], recv1.at[t, r], one_s.at[t, o - 1], one_r.at[t, r], (d, peer, c))

    def two_copy(t, o):
        peer = around(d, o, n_dp)
        return remote(half.at[t, peer], recv2.at[t, d], two_s.at[t, o - 1], two_r.at[t, d], (peer, r, c))

    def product(t):
        weight_copy(t).wait()
        out = lax.dot_general(cot[...], wt[t], CONTRACT_LAST, preferred_element_type=jnp.float32)
        for e in range(n_dp):
            for f in range(n_row):
                begin = (e * n_row + f) * own
                part[t, f, e] = out[begin:begin + own].astype(jnp.bfloat16)
        for o in range(1, n_row):
            one_copy(t, o).start()

    def sum_row(t):
        for o in range(1, n_row):
            peer = around(r, -o, n_row)
            ref = recv1.at[t, peer]
            remote(ref, ref, one_s.at[t, o - 1], one_r.at[t, peer], (d, around(r, o, n_row), c)).wait_recv()
        for e in range(n_dp):
            total = part[t, r, e].astype(jnp.float32)
            for o in range(1, n_row):
                total = total + recv1[t, around(r, -o, n_row), e].astype(jnp.float32)
            half[t, e] = total.astype(jnp.bfloat16)
        for o in range(1, n_dp):
            two_copy(t, o).start()

    def sum_dp(t):
        total = half[t, d].astype(jnp.float32)
        for o in range(1, n_dp):
            peer = around(d, -o, n_dp)
            ref = recv2.at[t, peer]
            remote(ref, ref, two_s.at[t, o - 1], two_r.at[t, peer], (around(d, o, n_dp), r, c)).wait_recv()
            total = total + recv2[t, peer].astype(jnp.float32)
        grad_hidden = total.astype(jnp.bfloat16).astype(jnp.float32)
        at = pl.ds(pl.multiple_of(t * tile, tile), tile)
        gate_f = gate[:, at].astype(jnp.float32)
        up_f = up[:, at].astype(jnp.float32)
        sigma = jax.nn.sigmoid(gate_f)
        grad_up[:, at] = (grad_hidden * (gate_f * sigma)).astype(jnp.bfloat16)
        grad_gate[:, at] = (grad_hidden * up_f * sigma * (1.0 + gate_f * (1.0 - sigma))).astype(jnp.bfloat16)

    @pl.loop(0, tiles)
    def _(t):
        product(t)

        @pl.when(t >= 1)
        def _():
            sum_row(t - 1)

        @pl.when(t >= 2)
        def _():
            sum_dp(t - 2)

    sum_row(tiles - 1)
    gather_end(hid_slot, hid_s, hid_r)
    hid_write = pltpu.make_async_copy(hid, hid_out, local_sem.at[3])
    hid_write.start()
    for o in range(1, n_col):
        peer = around(c, -o, n_col)
        remote(sums.at[peer], sums.at[peer], sum_s.at[o - 1], sum_r.at[peer], (d, r, around(c, o, n_col))).wait_recv()
    total = sums[0]
    for j in range(1, n_col):
        total = total + sums[j]
    scale_out[...] = jnp.sqrt(total[0:1]) / (jnp.sqrt(total[1:2]) + 1e-06)

    @pl.loop(max(tiles - 2, 0), tiles)
    def _(t):
        sum_dp(t)

    for copy in sent:
        copy.wait_send()

    @pl.loop(0, tiles)
    def _(t):
        for o in range(1, n_row):
            one_copy(t, o).wait_send()
        for o in range(1, n_dp):
            two_copy(t, o).wait_send()

    cot_write.wait()
    hid_write.wait()


def shards(n_dp, n_row, n_col, gate_pre, up_pre, grad_out, down_weight, basis, first_moment_in, second_moment_in):
    own, units = gate_pre.shape
    shard, columns = grad_out.shape
    row_ranks = first_moment_in.shape[0]
    ranks = row_ranks * n_col
    tokens = shard * n_col
    group = n_dp * n_row
    tile = width_of(units, 512)
    wide = width_of(columns, 512)
    tiles = units // tile
    sends = max(1, n_dp - 1 + n_dp * (n_row - 1))
    hops = n_col // 2
    bf16, f32 = jnp.bfloat16, jnp.float32
    vmem = pl.BlockSpec(memory_space=pltpu.VMEM)
    hbm = pl.BlockSpec(memory_space=pl.ANY)
    dma = pltpu.SemaphoreType.DMA
    grad_gate, grad_up, first_moment, second_moment, scale, cot, hid = pl.pallas_call(
        functools.partial(kernel, n_dp, n_row, n_col, tile, wide),
        out_shape=(
            jax.ShapeDtypeStruct((own, units), bf16),
            jax.ShapeDtypeStruct((own, units), bf16),
            jax.ShapeDtypeStruct((row_ranks, columns), f32),
            jax.ShapeDtypeStruct((row_ranks, columns), f32),
            jax.ShapeDtypeStruct((1, columns), f32),
            jax.ShapeDtypeStruct((tokens, columns), bf16),
            jax.ShapeDtypeStruct((tokens, units), bf16),
        ),
        in_specs=[vmem, vmem, hbm, hbm, hbm, vmem, vmem],
        out_specs=[vmem, vmem, vmem, vmem, vmem, hbm, hbm],
        scratch_shapes=[
            pltpu.VMEM((tokens, columns), bf16),
            pltpu.VMEM((tokens, units), bf16),
            pltpu.VMEM((ranks, units), bf16),
            pltpu.VMEM((tiles, tile, columns), bf16),
            pltpu.VMEM((tiles, n_row, n_dp, own, tile), bf16),
            pltpu.VMEM((tiles, n_row, n_dp, own, tile), bf16),
            pltpu.VMEM((tiles, n_dp, own, tile), bf16),
            pltpu.VMEM((tiles, n_dp, own, tile), bf16),
            pltpu.VMEM((n_col, row_ranks, own), bf16),
            pltpu.VMEM((n_col, row_ranks, own), bf16),
            pltpu.VMEM((group, row_ranks, own), bf16),
            pltpu.VMEM((n_col, 2, columns), f32),
            dma((4,)),
            dma((tiles,)),
            dma((2, hops)),
            dma((2, hops)),
            dma((sends,)),
            dma((group,)),
            dma((sends,)),
            dma((group,)),
            dma((n_col,)),
            dma((n_col,)),
            dma((sends,)),
            dma((group,)),
            dma((n_col,)),
            dma((n_col,)),
            dma((tiles, n_row)),
            dma((tiles, n_row)),
            dma((tiles, n_dp)),
            dma((tiles, n_dp)),
        ],
        compiler_params=pltpu.CompilerParams(
            collective_id=0, has_side_effects=True, vmem_limit_bytes=63 * 1024 * 1024
        ),
        cost_estimate=pl.CostEstimate(
            flops=2 * tokens * columns * units, bytes_accessed=2 * columns * units, transcendentals=0
        ),
    )(gate_pre, up_pre, grad_out, down_weight, basis, first_moment_in, second_moment_in)
    grad_weight = lax.dot_general(
        hid, cot, (((0,), (0,)), ((), ())), preferred_element_type=jnp.float32
    ).astype(jnp.bfloat16)
    scaled_grad = (grad_weight.astype(jnp.float32) * scale).astype(jnp.bfloat16)
    return (grad_gate, grad_up, scaled_grad, first_moment, second_moment)


def solution(mesh):
    split, by_col = P(("dp", "row"), "col"), P("col", ("dp", "row"))
    return jax.shard_map(
        functools.partial(shards, mesh.shape["dp"], mesh.shape["row"], mesh.shape["col"]),
        mesh=mesh,
        in_specs=(split, split, by_col, by_col, split, by_col, by_col),
        out_specs=(split, split, by_col, by_col, by_col),
        check_vma=False,
    )
```

time: 324 us -> 116 us (0.36)
  waiting for transfers between devices: 209 us -> 0 us
  Pallas kernels: 0 us -> 89.3 us
  blocking collectives: 40.6 us -> 0 us
  matrix products: 54.9 us -> 21.8 us
  between operations: 13.8 us -> 0.68 us
  other arithmetic: 3.54 us -> 0 us
    all_gather x3 -> x0, waiting for transfers between devices: 108 us -> none  [the longest x1 78.3 us: shards(): cotangent = lax.all_gather(grad_out, 'col', axis=0, tiled=True)]
    pallas_call x0 -> x1, Pallas kernels: none -> 89.3 us  [shards(): pl.pallas_call(functools.partial(kernel, n_dp, n_row, n_col, tile, wide),...]
    unnamed x6 -> x0, waiting for transfers between devices: 62.4 us -> none
    reduce_scatter x1 -> x0, waiting for transfers between devices: 38.9 us -> none  [shards(): lax.psum_scatter(lax.dot_general(out_rows, down_weight, (((1,), (1,)), ((...]
    psum x1 -> x0, blocking collectives: 34.8 us -> none  [shards(): lax.psum((jnp.sum(adapted * adapted, axis=0), jnp.sum(projected * project...]
    dot_general x4 -> x1, matrix products: 54.9 us -> 21.8 us  [shards(): lax.dot_general(hid, cot, (((0,), (0,)), ((), ())), preferred_element_typ...]
    all_gather x1 -> x0, blocking collectives: 5.79 us -> none  [shards(): every_token = lax.all_gather(own_tokens, ('dp', 'row'), axis=1, tiled=True)]
    convert_element_type x2 -> x0, other arithmetic: 3.52 us -> none  [the longest x1 3.51 us: shards(): hidden = (act_value * up_f).astype(jnp.bfloat16)]
  transfers between devices with their start and end apart: 5 -> 0, of which waited for: 4 -> 0; matrix products, arithmetic and copies ran while one was open for 3% -> 0% of each run, Pallas kernels for 0% -> 0%
where the time goes in v1:
time: 116 us
  Pallas kernels  89.3 us (77%)
  matrix products  21.8 us (19%)
  local copies, waits for them, and re-layouts  3.8 us (3%)
    pallas_call x1, Pallas kernels, shards(): pl.pallas_call(functools.partial(kernel, n_dp, n_row, n_col, tile, wide),...  89.3 us
    dot_general x1, matrix products, shards(): lax.dot_general(hid, cot, (((0,), (0,)), ((), ())), preferred_element_typ...  21.8 us
    unnamed x12, local copies, waits for them, and re-layouts  3.8 us

profile of v1, /device:TPU:0, one launch (start us, length us, event | category | flops | bytes accessed | tf_op | source)
XLA Modules:
  0.0 115.6 jit_solution(4609766789863962651)
XLA Ops:
  0.6 89.3 %shard_map.110 = (bf16[128,3584]{1,0:T(8,128)(2,1)}, bf16[128,3584]{1,0:T(8,128)(2,1)}, f32[64,4096]{1,0:T(8,128)}, f32[64,4096]{1,0:T(8,128)}, f32[1,4096]{1,0:...) custom-call(bf16[128,3584]{1,0:T(8,128)(2,1)} %gate.1, bf16[128,3584]{1,0:T(8,128)(2,1)} %up.1, ...), custom_call_target="tpu_custom_call" | custom-call | flops 15032385536 | bytes 29360128 | tf_op jit(solution)/shard_map/pallas_call | solution.py:327
  90.0 0.0 copy-start.3
  90.0 0.0 copy-start.2
  90.0 0.0 copy-start.1
  90.0 0.0 copy-start
  90.0 21.8 %multiply_convert_fusion = bf16[3584,4096]{1,0:T(8,128)(2,1)} fusion(f32[4096]{0:T(1024)} %bitcast.3, bf16[512,3584]{1,0:T(8,128)(2,1)} %get-tuple-element.14, bf16[512,4096]{1,0:T(8,128)(2,1)} %get-tuple-element.15), kind=kOutput, calls=%fused_computation | convolution fusion | flops 15091105792 | bytes 37240832 | tf_op jit(solution)/shard_map/dot_general | solution.py:379
  111.8 0.0 copy-done.3
  111.8 0.9 copy.16
  112.7 0.0 copy-done.2
  112.7 0.9 copy.17
  113.7 0.0 copy-done.1
  113.7 1.0 copy.18
  114.6 0.0 copy-done
  114.6 1.0 copy.19
Async XLA Ops:
  90.0 21.8 %copy-start.3 = (bf16[128,3584]{1,0:T(8,128)(2,1)S(1)}, bf16[128,3584]{1,0:T(8,128)(2,1)}, u32[]{:S(2)}) copy-start(bf16[128,3584]{1,0:T(8,128)(2,1)} %get-tuple-element.24) | copy-start | bytes 2752516
  90.0 22.8 %copy-start.2 = (bf16[128,3584]{1,0:T(8,128)(2,1)S(1)}, bf16[128,3584]{1,0:T(8,128)(2,1)}, u32[]{:S(2)}) copy-start(bf16[128,3584]{1,0:T(8,128)(2,1)} %get-tuple-element.25) | copy-start | bytes 2752516
  90.0 23.7 %copy-start.1 = (f32[64,4096]{1,0:T(8,128)S(1)}, f32[64,4096]{1,0:T(8,128)}, u32[]{:S(2)}) copy-start(f32[64,4096]{1,0:T(8,128)} %get-tuple-element.27) | copy-start | bytes 3145732
  90.0 24.6 %copy-start = (f32[64,4096]{1,0:T(8,128)S(1)}, f32[64,4096]{1,0:T(8,128)}, u32[]{:S(2)}) copy-start(f32[64,4096]{1,0:T(8,128)} %get-tuple-element.28) | copy-start | bytes 3145732

commit v2 on v1

--- a/solution.py
+++ b/solution.py
@@ -185,100 +185,154 @@
     for o in range(1, n_col):
         peer = around(c, o, n_col)
         start(remote(tok_send.at[peer], tok_recv.at[c], tk_s.at[o - 1], tk_r.at[c], (d, r, peer)))
+    def token_sum():
+        total = tok_send[c].astype(jnp.float32)
+        for o in range(1, n_col):
+            peer = around(c, -o, n_col)
+            remote(tok_recv.at[peer], tok_recv.at[peer], tk_s.at[o - 1], tk_r.at[peer], (d, r, around(c, o, n_col))).wait_recv()
+            total = total + tok_recv[peer].astype(jnp.float32)
+        tok_all[k] = total.astype(jnp.bfloat16)
+        gather_start(tok_slot(k), tok_slot, tg_s, tg_r)
+
+    def project():
+        token_all = jnp.concatenate([tok_all[j] for j in range(group)], axis=1)
+
+        @pl.loop(0, columns // wide)
+        def _(j):
+            at = pl.ds(pl.multiple_of(j * wide, wide), wide)
+            projected = jnp.dot(token_all, cot[:, at], preferred_element_type=jnp.float32)
+            first = 0.9 * first_in[:, at] + 0.1 * projected
+            second = 0.999 * second_in[:, at] + 0.001 * projected * projected
+            adapted = first / first_fix / (jnp.sqrt(second / second_fix) + 1e-06)
+            first_out[:, at] = first
+            second_out[:, at] = second
+            sums[c, 0:1, at] = jnp.sum(adapted * adapted, axis=0, keepdims=True)
+            sums[c, 1:2, at] = jnp.sum(projected * projected, axis=0, keepdims=True)
+
+        for o in range(1, n_col):
+            start(remote(sums.at[c], sums.at[c], sum_s.at[o - 1], sum_r.at[c], (d, r, around(c, o, n_col))))
+
+    per = own // shard
+    early_steps = hops // 2
+    order = [0]
+    for o in range(1, hops):
+        order += [-o, o]
+    order += [hops]
+    early = 2 * early_steps + 1
+    groups = (range(0, early), range(early, n_col))
+
+    def place(i):
+        q = ring_col(order[i])
+        block = lax.div(q, per)
+        return q, lax.div(block, n_row), lax.rem(block, n_row), lax.rem(q, per)
+
+    def one_copy(t, i):
+        q, e, f, sub = place(i)
+        slot = e * per + sub
+        return remote(part.at[t, i], recv1.at[t, r, slot], one_s.at[t, i], one_r.at[t, r, slot], (d, f, c))
+
+    def two_copy(t, i):
+        q, e, f, sub = place(i)
+        slot = e * per + sub
+        return remote(half.at[t, slot], recv2.at[t, d, sub], two_s.at[t, slot], two_r.at[t, d, sub], (e, r, c))
+
+    def product(g, t):
+        if g == 0:
+            weight_copy(t).wait()
+        slots = groups[g]
+        left = jnp.concatenate(
+            [rows_of(ring_col(order[i]))[...] for i in slots], axis=0)
+        out = lax.dot_general(left, wt[t], CONTRACT_LAST, preferred_element_type=jnp.float32)
+        for n, i in enumerate(slots):
+            part[t, i] = out[n * shard:(n + 1) * shard].astype(jnp.bfloat16)
+        for i in slots:
+            f = place(i)[2]
+
+            @pl.when(f != r)
+            def _():
+                one_copy(t, i).start()
+
+    def sum_row(g, t):
+        for i in groups[g]:
+            q, e, f, sub = place(i)
+            slot = e * per + sub
+
+            @pl.when(f == r)
+            def _():
+                total = part[t, i].astype(jnp.float32)
+                for o in range(1, n_row):
+                    peer = around(r, -o, n_row)
+                    ref = recv1.at[t, peer, slot]
+                    remote(ref, ref, one_s.at[t, i], one_r.at[t, peer, slot], (d, around(r, o, n_row), c)).wait_recv()
+                    total = total + recv1[t, peer, slot].astype(jnp.float32)
+                half[t, slot] = total.astype(jnp.bfloat16)
+
+                @pl.when(e != d)
+                def _():
+                    two_copy(t, i).start()
+
+    def sum_dp(g, t):
+        for i in groups[g]:
+            q, e, f, sub = place(i)
+
+            @pl.when(e * n_row + f == k)
+            def _():
+                total = half[t, e * per + sub].astype(jnp.float32)
+                for o in range(1, n_dp):
+                    peer = around(d, -o, n_dp)
+                    ref = recv2.at[t, peer, sub]
+                    remote(ref, ref, two_s.at[t, 0], two_r.at[t, peer, sub], (around(d, o, n_dp), r, c)).wait_recv()
+                    total = total + recv2[t, peer, sub].astype(jnp.float32)
+                grad_hidden = total.astype(jnp.bfloat16).astype(jnp.float32)
+                at = pl.ds(pl.multiple_of(t * tile, tile), tile)
+                rows = pl.ds(pl.multiple_of(sub * shard, shard), shard)
+                gate_f = gate[rows, at].astype(jnp.float32)
+                up_f = up[rows, at].astype(jnp.float32)
+                sigma = jax.nn.sigmoid(gate_f)
+                grad_up[rows, at] = (grad_hidden * (gate_f * sigma)).astype(jnp.bfloat16)
+                grad_gate[rows, at] = (
+                    grad_hidden * up_f * sigma * (1.0 + gate_f * (1.0 - sigma))).astype(jnp.bfloat16)
+
+    def early_tiles(begin, end):
+        @pl.loop(begin, end)
+        def _(t):
+            product(0, t)
+
+            @pl.when(t >= 1)
+            def _():
+                sum_row(0, t - 1)
+
+    def late_tiles(begin, end):
+        @pl.loop(begin, end)
+        def _(t):
+            product(1, t)
+
+            @pl.when(t >= 1)
+            def _():
+                sum_row(1, t - 1)
+
+            sum_dp(0, t)
+
+    own_cot.wait()
+    while step <= early_steps:
+        ring_step()
+    cut = min(4, tiles)
+    early_tiles(0, cut)
     ring_step()
-    total = tok_send[c].astype(jnp.float32)
-    for o in range(1, n_col):
-        peer = around(c, -o, n_col)
-        remote(tok_recv.at[peer], tok_recv.at[peer], tk_s.at[o - 1], tk_r.at[peer], (d, r, around(c, o, n_col))).wait_recv()
-        total = total + tok_recv[peer].astype(jnp.float32)
-    tok_all[k] = total.astype(jnp.bfloat16)
-    gather_start(tok_slot(k), tok_slot, tg_s, tg_r)
-    ring_step()
-    gather_pass(tok_slot, tg_s, tg_r)
-    gather_end(tok_slot, tg_s, tg_r)
+    token_sum()
+    early_tiles(cut, tiles)
     while step <= hops:
         ring_step()
-    own_cot.wait()
     cot_write = pltpu.make_async_copy(cot, cot_out, local_sem.at[2])
     cot_write.start()
+    gather_pass(tok_slot, tg_s, tg_r)
     gather_pass(hid_slot, hid_s, hid_r)
-
-    token_all = jnp.concatenate([tok_all[j] for j in range(group)], axis=1)
-
-    @pl.loop(0, columns // wide)
-    def _(j):
-        at = pl.ds(pl.multiple_of(j * wide, wide), wide)
-        projected = jnp.dot(token_all, cot[:, at], preferred_element_type=jnp.float32)
-        first = 0.9 * first_in[:, at] + 0.1 * projected
-        second = 0.999 * second_in[:, at] + 0.001 * projected * projected
-        adapted = first / first_fix / (jnp.sqrt(second / second_fix) + 1e-06)
-        first_out[:, at] = first
-        second_out[:, at] = second
-        sums[c, 0:1, at] = jnp.sum(adapted * adapted, axis=0, keepdims=True)
-        sums[c, 1:2, at] = jnp.sum(projected * projected, axis=0, keepdims=True)
-
-    for o in range(1, n_col):
-        start(remote(sums.at[c], sums.at[c], sum_s.at[o - 1], sum_r.at[c], (d, r, around(c, o, n_col))))
-
-    def one_copy(t, o):
-        peer = around(r, o, n_row)
-        return remote(part.at[t, peer], recv1.at[t, r], one_s.at[t, o - 1], one_r.at[t, r], (d, peer, c))
-
-    def two_copy(t, o):
-        peer = around(d, o, n_dp)
-        return remote(half.at[t, peer], recv2.at[t, d], two_s.at[t, o - 1], two_r.at[t, d], (peer, r, c))
-
-    def product(t):
-        weight_copy(t).wait()
-        out = lax.dot_general(cot[...], wt[t], CONTRACT_LAST, preferred_element_type=jnp.float32)
-        for e in range(n_dp):
-            for f in range(n_row):
-                begin = (e * n_row + f) * own
-                part[t, f, e] = out[begin:begin + own].astype(jnp.bfloat16)
-        for o in range(1, n_row):
-            one_copy(t, o).start()
-
-    def sum_row(t):
-        for o in range(1, n_row):
-            peer = around(r, -o, n_row)
-            ref = recv1.at[t, peer]
-            remote(ref, ref, one_s.at[t, o - 1], one_r.at[t, peer], (d, around(r, o, n_row), c)).wait_recv()
-        for e in range(n_dp):
-            total = part[t, r, e].astype(jnp.float32)
-            for o in range(1, n_row):
-                total = total + recv1[t, around(r, -o, n_row), e].astype(jnp.float32)
-            half[t, e] = total.astype(jnp.bfloat16)
-        for o in range(1, n_dp):
-            two_copy(t, o).start()
-
-    def sum_dp(t):
-        total = half[t, d].astype(jnp.float32)
-        for o in range(1, n_dp):
-            peer = around(d, -o, n_dp)
-            ref = recv2.at[t, peer]
-            remote(ref, ref, two_s.at[t, o - 1], two_r.at[t, peer], (around(d, o, n_dp), r, c)).wait_recv()
-            total = total + recv2[t, peer].astype(jnp.float32)
-        grad_hidden = total.astype(jnp.bfloat16).astype(jnp.float32)
-        at = pl.ds(pl.multiple_of(t * tile, tile), tile)
-        gate_f = gate[:, at].astype(jnp.float32)
-        up_f = up[:, at].astype(jnp.float32)
-        sigma = jax.nn.sigmoid(gate_f)
-        grad_up[:, at] = (grad_hidden * (gate_f * sigma)).astype(jnp.bfloat16)
-        grad_gate[:, at] = (grad_hidden * up_f * sigma * (1.0 + gate_f * (1.0 - sigma))).astype(jnp.bfloat16)
-
-    @pl.loop(0, tiles)
-    def _(t):
-        product(t)
-
-        @pl.when(t >= 1)
-        def _():
-            sum_row(t - 1)
-
-        @pl.when(t >= 2)
-        def _():
-            sum_dp(t - 2)
-
-    sum_row(tiles - 1)
+    sum_row(0, tiles - 1)
+    gather_end(tok_slot, tg_s, tg_r)
+    late_tiles(0, cut)
+    project()
+    late_tiles(cut, tiles)
+    sum_row(1, tiles - 1)
     gather_end(hid_slot, hid_s, hid_r)
     hid_write = pltpu.make_async_copy(hid, hid_out, local_sem.at[3])
     hid_write.start()
@@ -290,19 +344,25 @@
         total = total + sums[j]
     scale_out[...] = jnp.sqrt(total[0:1]) / (jnp.sqrt(total[1:2]) + 1e-06)
 
-    @pl.loop(max(tiles - 2, 0), tiles)
+    @pl.loop(0, tiles)
     def _(t):
-        sum_dp(t)
+        sum_dp(1, t)
 
     for copy in sent:
         copy.wait_send()
 
     @pl.loop(0, tiles)
     def _(t):
-        for o in range(1, n_row):
-            one_copy(t, o).wait_send()
-        for o in range(1, n_dp):
-            two_copy(t, o).wait_send()
+        for i in range(n_col):
+            q, e, f, sub = place(i)
+
+            @pl.when(f != r)
+            def _():
+                one_copy(t, i).wait_send()
+
+            @pl.when((f == r) & (e != d))
+            def _():
+                two_copy(t, i).wait_send()
 
     cot_write.wait()
     hid_write.wait()
@@ -320,6 +380,7 @@
     tiles = units // tile
     sends = max(1, n_dp - 1 + n_dp * (n_row - 1))
     hops = n_col // 2
+    per = own // shard
     bf16, f32 = jnp.bfloat16, jnp.float32
     vmem = pl.BlockSpec(memory_space=pltpu.VMEM)
     hbm = pl.BlockSpec(memory_space=pl.ANY)
@@ -342,10 +403,10 @@
             pltpu.VMEM((tokens, units), bf16),
             pltpu.VMEM((ranks, units), bf16),
             pltpu.VMEM((tiles, tile, columns), bf16),
-            pltpu.VMEM((tiles, n_row, n_dp, own, tile), bf16),
-            pltpu.VMEM((tiles, n_row, n_dp, own, tile), bf16),
-            pltpu.VMEM((tiles, n_dp, own, tile), bf16),
-            pltpu.VMEM((tiles, n_dp, own, tile), bf16),
+            pltpu.VMEM((tiles, n_col, shard, tile), bf16),
+            pltpu.VMEM((tiles, n_row, n_dp * per, shard, tile), bf16),
+            pltpu.VMEM((tiles, n_dp * per, shard, tile), bf16),
+            pltpu.VMEM((tiles, n_dp, per, shard, tile), bf16),
             pltpu.VMEM((n_col, row_ranks, own), bf16),
             pltpu.VMEM((n_col, row_ranks, own), bf16),
             pltpu.VMEM((group, row_ranks, own), bf16),
@@ -364,10 +425,10 @@
             dma((group,)),
             dma((n_col,)),
             dma((n_col,)),
-            dma((tiles, n_row)),
-            dma((tiles, n_row)),
-            dma((tiles, n_dp)),
-            dma((tiles, n_dp)),
+            dma((tiles, n_col)),
+            dma((tiles, n_row, n_dp * per)),
+            dma((tiles, n_dp * per)),
+            dma((tiles, n_dp, per)),
         ],
         compiler_params=pltpu.CompilerParams(
             collective_id=0, has_side_effects=True, vmem_limit_bytes=63 * 1024 * 1024

time: 116 us -> 112 us (0.966); the launches traced: 116 us -> 110 us
  Pallas kernels: 89.3 us -> 84.1 us
    pallas_call x1, Pallas kernels: 89.3 us -> 84.1 us  [shards(): pl.pallas_call(functools.partial(kernel, n_dp, n_row, n_col, tile, wide),...]
where the time goes in v2:
time: 112 us; the launch traced here: 110 us
  Pallas kernels  84.1 us (75%)
  matrix products  21.8 us (19%)
  local copies, waits for them, and re-layouts  3.8 us (3%)
    pallas_call x1, Pallas kernels, shards(): pl.pallas_call(functools.partial(kernel, n_dp, n_row, n_col, tile, wide),...  84.1 us
    dot_general x1, matrix products, shards(): lax.dot_general(hid, cot, (((0,), (0,)), ((), ())), preferred_element_typ...  21.8 us
    unnamed x12, local copies, waits for them, and re-layouts  3.8 us

profile of v2, /device:TPU:0, one launch (start us, length us, event | category | flops | bytes accessed | tf_op | source)
XLA Modules:
  0.0 110.4 jit_solution(15257322477115118356)
XLA Ops:
  0.6 84.1 %shard_map.110 = (bf16[128,3584]{1,0:T(8,128)(2,1)}, bf16[128,3584]{1,0:T(8,128)(2,1)}, f32[64,4096]{1,0:T(8,128)}, f32[64,4096]{1,0:T(8,128)}, f32[1,4096]{1,0:...) custom-call(bf16[128,3584]{1,0:T(8,128)(2,1)} %gate.1, bf16[128,3584]{1,0:T(8,128)(2,1)} %up.1, ...), custom_call_target="tpu_custom_call" | custom-call | flops 15032385536 | bytes 29360128 | tf_op jit(solution)/shard_map/pallas_call | solution.py:388
  84.7 0.0 copy-start.3
  84.7 0.0 copy-start.2
  84.7 0.0 copy-start.1
  84.8 0.0 copy-start
  84.8 21.8 %multiply_convert_fusion = bf16[3584,4096]{1,0:T(8,128)(2,1)} fusion(f32[4096]{0:T(1024)} %bitcast.3, bf16[512,3584]{1,0:T(8,128)(2,1)} %get-tuple-element.14, bf16[512,4096]{1,0:T(8,128)(2,1)} %get-tuple-element.15), kind=kOutput, calls=%fused_computation | convolution fusion | flops 15091105792 | bytes 37240832 | tf_op jit(solution)/shard_map/dot_general | solution.py:440
  106.6 0.0 copy-done.3
  106.6 0.9 copy.16
  107.5 0.0 copy-done.2
  107.5 0.9 copy.17
  108.4 0.0 copy-done.1
  108.4 1.0 copy.18
  109.4 0.0 copy-done
  109.4 1.0 copy.19
Async XLA Ops:
  84.7 21.8 %copy-start.3 = (bf16[128,3584]{1,0:T(8,128)(2,1)S(1)}, bf16[128,3584]{1,0:T(8,128)(2,1)}, u32[]{:S(2)}) copy-start(bf16[128,3584]{1,0:T(8,128)(2,1)} %get-tuple-element.24) | copy-start | bytes 2752516
  84.7 22.8 %copy-start.2 = (bf16[128,3584]{1,0:T(8,128)(2,1)S(1)}, bf16[128,3584]{1,0:T(8,128)(2,1)}, u32[]{:S(2)}) copy-start(bf16[128,3584]{1,0:T(8,128)(2,1)} %get-tuple-element.25) | copy-start | bytes 2752516
  84.7 23.7 %copy-start.1 = (f32[64,4096]{1,0:T(8,128)S(1)}, f32[64,4096]{1,0:T(8,128)}, u32[]{:S(2)}) copy-start(f32[64,4096]{1,0:T(8,128)} %get-tuple-element.27) | copy-start | bytes 3145732
  84.8 24.6 %copy-start = (f32[64,4096]{1,0:T(8,128)S(1)}, f32[64,4096]{1,0:T(8,128)}, u32[]{:S(2)}) copy-start(f32[64,4096]{1,0:T(8,128)} %get-tuple-element.28) | copy-start | bytes 3145732

commit v3 on v2

--- a/solution.py
+++ b/solution.py
@@ -53,6 +53,7 @@
     row_ranks = ranks // n_col
     tiles = units // tile
     hops = n_col // 2
+    early_steps = hops // 2
 
     def around(me, offset, n):
         return lax.rem(me + offset + n, n)
@@ -174,6 +175,8 @@
     ring_step()
     gather_pass(basis_slot, bas_s, bas_r)
     gather_start(hid_slot(k), hid_slot, hid_s, hid_r)
+    if early_steps > 1:
+        ring_step()
     own_basis.wait()
     gather_end(basis_slot, bas_s, bas_r)
 
@@ -213,7 +216,6 @@
             start(remote(sums.at[c], sums.at[c], sum_s.at[o - 1], sum_r.at[c], (d, r, around(c, o, n_col))))
 
     per = own // shard
-    early_steps = hops // 2
     order = [0]
     for o in range(1, hops):
         order += [-o, o]
@@ -316,7 +318,7 @@
     own_cot.wait()
     while step <= early_steps:
         ring_step()
-    cut = min(4, tiles)
+    cut = min(3, tiles)
     early_tiles(0, cut)
     ring_step()
     token_sum()

time: 112 us -> 110 us (0.982)
  Pallas kernels: 84.1 us -> 81.3 us
    pallas_call x1, Pallas kernels: 84.1 us -> 81.3 us  [shards(): pl.pallas_call(functools.partial(kernel, n_dp, n_row, n_col, tile, wide),...]
where the time goes in v3:
time: 110 us; the launch traced here: 108 us
  Pallas kernels  81.3 us (74%)
  matrix products  21.8 us (20%)
  local copies, waits for them, and re-layouts  3.8 us (3%)
    pallas_call x1, Pallas kernels, shards(): pl.pallas_call(functools.partial(kernel, n_dp, n_row, n_col, tile, wide),...  81.3 us
    dot_general x1, matrix products, shards(): lax.dot_general(hid, cot, (((0,), (0,)), ((), ())), preferred_element_typ...  21.8 us
    unnamed x12, local copies, waits for them, and re-layouts  3.8 us

profile of v3, /device:TPU:0, one launch (start us, length us, event | category | flops | bytes accessed | tf_op | source)
XLA Modules:
  0.0 107.5 jit_solution(18171372401096950268)
XLA Ops:
  0.6 81.3 %shard_map.110 = (bf16[128,3584]{1,0:T(8,128)(2,1)}, bf16[128,3584]{1,0:T(8,128)(2,1)}, f32[64,4096]{1,0:T(8,128)}, f32[64,4096]{1,0:T(8,128)}, f32[1,4096]{1,0:...) custom-call(bf16[128,3584]{1,0:T(8,128)(2,1)} %gate.1, bf16[128,3584]{1,0:T(8,128)(2,1)} %up.1, ...), custom_call_target="tpu_custom_call" | custom-call | flops 15032385536 | bytes 29360128 | tf_op jit(solution)/shard_map/pallas_call | solution.py:390
  81.9 0.0 copy-start.3
  81.9 0.0 copy-start.2
  81.9 0.0 copy-start.1
  81.9 0.0 copy-start
  81.9 21.8 %multiply_convert_fusion = bf16[3584,4096]{1,0:T(8,128)(2,1)} fusion(f32[4096]{0:T(1024)} %bitcast.3, bf16[512,3584]{1,0:T(8,128)(2,1)} %get-tuple-element.14, bf16[512,4096]{1,0:T(8,128)(2,1)} %get-tuple-element.15), kind=kOutput, calls=%fused_computation | convolution fusion | flops 15091105792 | bytes 37240832 | tf_op jit(solution)/shard_map/dot_general | solution.py:442
  103.7 0.0 copy-done.3
  103.7 0.9 copy.16
  104.7 0.0 copy-done.2
  104.7 0.9 copy.17
  105.6 0.0 copy-done.1
  105.6 1.0 copy.18
  106.6 0.0 copy-done
  106.6 1.0 copy.19
Async XLA Ops:
  81.9 21.8 %copy-start.3 = (bf16[128,3584]{1,0:T(8,128)(2,1)S(1)}, bf16[128,3584]{1,0:T(8,128)(2,1)}, u32[]{:S(2)}) copy-start(bf16[128,3584]{1,0:T(8,128)(2,1)} %get-tuple-element.24) | copy-start | bytes 2752516
  81.9 22.8 %copy-start.2 = (bf16[128,3584]{1,0:T(8,128)(2,1)S(1)}, bf16[128,3584]{1,0:T(8,128)(2,1)}, u32[]{:S(2)}) copy-start(bf16[128,3584]{1,0:T(8,128)(2,1)} %get-tuple-element.25) | copy-start | bytes 2752516
  81.9 23.7 %copy-start.1 = (f32[64,4096]{1,0:T(8,128)S(1)}, f32[64,4096]{1,0:T(8,128)}, u32[]{:S(2)}) copy-start(f32[64,4096]{1,0:T(8,128)} %get-tuple-element.27) | copy-start | bytes 3145732
  81.9 24.6 %copy-start = (f32[64,4096]{1,0:T(8,128)S(1)}, f32[64,4096]{1,0:T(8,128)}, u32[]{:S(2)}) copy-start(f32[64,4096]{1,0:T(8,128)} %get-tuple-element.28) | copy-start | bytes 3145732
